TPU v7x, 512 devices: a whole 4x8x8 slice. The times are simulated.
512 devices in a mesh: ctx: 64 (over x, z, core), head: 8 (over y).
Axes of the slice: x: 4, y: 8, z: 8, core: 2. Of those that a mesh axis runs over, the one named last changes fastest.
Arguments:
- qkv: bfloat16 [1, 65536, 6144], P(None, ('ctx', 'head')), may hold values from -6 to 6
- grad_out: bfloat16 [1, 65536, 2048], P(None, ('ctx', 'head')), may hold values from -6 to 6
- w_qkv: bfloat16 [2048, 6144], P('ctx', 'head'), may hold values from -0.078125 to 0.078125
Outputs:
- grad_input: float32 [1, 65536, 2048], P(None, ('ctx', 'head'))
All inputs are finite; a program needn't handle non-finite values.
Results may differ from a plain program's by a relative error of at most 0.02.
Values may be sent and summed in bfloat16 or wider, within the bound.
A program may use at most 128 MiB of HBM per device.

v0:
```python
import math
import jax
import jax.numpy as jnp
from jax import lax
from jax.sharding import PartitionSpec as P

DH = 128


def carried_in(x, axis, join, neutral, backward):
    count = lax.axis_size(axis)
    place = lax.axis_index(axis)
    ahead = count - 1 - place if backward else place
    gathered = lax.all_gather(x.astype(jnp.bfloat16), axis)
    state = jnp.zeros_like(x) + jnp.asarray(neutral, x.dtype)

    def one(step, state):
        source = count - 1 - step if backward else step
        return join(state, lax.dynamic_index_in_dim(gathered, source, 0, False).astype(x.dtype))

    return lax.fori_loop(0, ahead, one, state)


def combine_sum(earlier, later):
    return earlier + later


def per_device(qkv, grad_out, w_qkv):
    highest = lax.Precision.HIGHEST
    whole_weight = lax.all_gather(w_qkv, "ctx", axis=0, tiled=True)
    local_qkv, local_grad = (
        lax.all_to_all(qkv, "head", split_axis=2, concat_axis=1, tiled=True),
        lax.all_to_all(grad_out, "head", split_axis=2, concat_axis=1, tiled=True),
    )
    num_seqs, block_len, width3 = local_qkv.shape
    heads_here = width3 // (3 * DH)
    factor = 1.0 / math.sqrt(DH * block_len * lax.axis_size("ctx"))
    blocks = local_qkv.reshape(num_seqs, block_len, heads_here, 3, DH)
    query_rows = blocks[:, :, :, 0]
    key_rows = blocks[:, :, :, 1]
    value_rows = blocks[:, :, :, 2]
    grad_rows = local_grad.reshape(num_seqs, block_len, heads_here, DH)
    kv_own = jnp.einsum("sthd,sthe->shde", key_rows, value_rows, preferred_element_type=jnp.float32)
    qg_own = jnp.einsum(
        "sthd,sthe->shde", query_rows, grad_rows, preferred_element_type=jnp.float32
    )
    empty_state = jnp.zeros_like(kv_own)
    kv_before = carried_in(kv_own, "ctx", combine_sum, empty_state, False)
    qg_after = carried_in(qg_own, "ctx", combine_sum, empty_state, True)
    positions = lax.broadcasted_iota(jnp.int32, (block_len, block_len), 0)
    columns = lax.broadcasted_iota(jnp.int32, (block_len, block_len), 1)
    causal = (positions >= columns).astype(jnp.float32)
    scores_gv = (
        jnp.einsum("sthe,suhe->shtu", grad_rows, value_rows, preferred_element_type=jnp.float32)
        * causal
    )
    scores_qk = (
        jnp.einsum("sthd,suhd->shtu", query_rows, key_rows, preferred_element_type=jnp.float32)
        * causal
    )
    key_wide = key_rows.astype(jnp.float32)
    grad_wide = grad_rows.astype(jnp.float32)
    grad_q = jnp.einsum("shtu,suhd->sthd", scores_gv, key_wide, precision=highest) + jnp.einsum(
        "sthe,shde->sthd", grad_wide, kv_before, precision=highest
    )
    query_wide = query_rows.astype(jnp.float32)
    value_wide = value_rows.astype(jnp.float32)
    grad_k = jnp.einsum("shtu,sthd->suhd", scores_gv, query_wide, precision=highest) + jnp.einsum(
        "suhe,shde->suhd", value_wide, qg_after, precision=highest
    )
    grad_v = jnp.einsum("shtu,sthe->suhe", scores_qk, grad_wide, precision=highest) + jnp.einsum(
        "suhd,shde->suhe", key_wide, qg_after, precision=highest
    )
    gradients = (
        (jnp.stack([grad_q, grad_k, grad_v], axis=3) * factor)
        .astype(jnp.bfloat16)
        .reshape(num_seqs, block_len, width3)
    )
    own_rows = lax.psum_scatter(
        jnp.einsum(
            "stf,df->tsd", gradients, whole_weight, preferred_element_type=jnp.float32
        ).astype(jnp.bfloat16),
        "head",
        scatter_dimension=0,
        tiled=True,
    ).astype(jnp.float32)
    return jnp.transpose(own_rows, (1, 0, 2))


def solution(mesh):
    in_specs = (P(None, ("ctx", "head"), None), P(None, ("ctx", "head"), None), P("ctx", "head"))
    out_specs = P(None, ("ctx", "head"), None)
    return jax.shard_map(
        per_device, mesh=mesh, in_specs=in_specs, out_specs=out_specs, check_vma=False
    )
```

profile of v0, /device:TPU:1, one launch (start us, length us, event | category | flops | bytes accessed | tf_op | source)
XLA Modules:
  0.0 456.7 jit_solution(5175588874633387678)
XLA Ops:
  6.5 2.3 copy.42
  9.4 11.4 %reduce = bf16[2048,128]{1,0:T(8,128)(2,1)S(1)} reduce(bf16[2048,1,128]{2,1,0:T(2,128)(2,1)S(1)} %bitcast.109, bf16[]{:T(256)} %broadcast.9), dimensions={1}, to_apply=%bitcast.91.reduce_sub_computation | reduce | bytes 1048578
  21.8 7.7 %all-to-all-start = ((bf16[8,2,16384]{2,1,0:T(2,128)(2,1)}), bf16[8,2,16384]{2,1,0:T(2,128)(2,1)}, u32[]{:S(2)}, u32[]{:S(2)}) async-start(bf16[8,2,16384]{2,1,0:T(2,128)(2,1)} %reshape.156), calls=%async_computation | async-start | bytes 1048576 | tf_op jit(solution)/shard_map/all_to_all | solution.py:33
  29.4 6.8 %copy.44 = bf16[1,128,6144]{1,0,2:T(2,128)(2,1)S(1)} copy(bf16[1,128,6144]{2,1,0:T(8,128)(2,1)} %param.7) | data formatting | bytes 3145728 | tf_op args[0]
  36.2 34.3 %reduce.1 = bf16[6144,128]{1,0:T(8,128)(2,1)} reduce(bf16[6144,1,128]{2,1,0:T(2,128)(2,1)S(1)} %bitcast.105, bf16[]{:T(256)} %broadcast.9), dimensions={1}, to_apply=%bitcast.93.reduce_sub_computation | reduce | bytes 3145730
  70.6 3.7 reshape.158
  74.3 6.6 %all-to-all-start.1 = ((bf16[8,2,49152]{2,1,0:T(2,128)(2,1)}), bf16[8,2,49152]{2,1,0:T(2,128)(2,1)}, u32[]{:S(2)}, u32[]{:S(2)}) async-start(bf16[8,2,49152]{2,1,0:T(2,128)(2,1)} %reshape.158), calls=%async_computation.1 | async-start | bytes 3145728 | tf_op jit(solution)/shard_map/all_to_all | solution.py:32
  81.2 2.2 reshape.157
  84.8 33.7 %all-to-all-done.1 = bf16[8,2,49152]{2,1,0:T(2,128)(2,1)} async-done(((bf16[8,2,49152]{2,1,0:T(2,128)(2,1)}), bf16[8,2,49152]{2,1,0:T(2,128)(2,1)}, u32[]{:S(2)}, u32[]{:S(2)}) %all-to-all-start.1) | async-done | bytes 1572896 | tf_op jit(solution)/shard_map/all_to_all | solution.py:32
  118.5 4.7 %reshape.159 = bf16[6144,1,128]{2,1,0:T(2,128)(2,1)S(1)} reshape(bf16[8,2,49152]{2,1,0:T(2,128)(2,1)} %all-to-all-done.1) | data formatting | bytes 3145728
  123.4 2.2 copy.45
  125.6 2.5 reshape.145
  131.4 4.5 fusion.24
  137.2 4.3 fusion.14
  141.5 5.0 %fusion.11 = f32[2,128,1024]{2,1,0:T(8,128)S(1)} fusion(f32[2,1024,1024]{2,1,0:T(8,128)S(1)} %fusion.23, f32[1024,1024]{1,0:T(8,128)S(1)} %fusion.9, bf16[1,1024,2,3,128]{1,4,3,2,0:T(8,128)(2,1)S(1)} %reshape.145), kind=kOutput, calls=%fused_computation.16 | convolution fusion | flops 3223322624 | bytes 14155776 | tf_op jit(solution)/shard_map/shtu,suhd->sthd/dot_general | solution.py:63
  146.6 8.0 %fusion.17 = f32[2,128,1024]{2,1,0:T(8,128)} fusion(bf16[1024,2,128]{0,2,1:T(8,128)(2,1)S(1)} %copy-done, f32[2,1024,1024]{2,1,0:T(8,128)} %fusion.24, f32[1024,1024]{1,0:T(8,128)S(1)} %fusion.9), kind=kOutput, calls=%fused_computation.18 | convolution fusion | flops 3223322624 | bytes 14155776 | tf_op jit(solution)/shard_map/shtu,sthe->suhe/dot_general | solution.py:71
  154.6 62.5 %all-gather.10.cloned.1.call-done = bf16[128,128,128]{2,1,0:T(8,128)(2,1)} async-done(((bf16[2,128,128]{2,1,0:T(8,128)(2,1)}), bf16[128,128,128]{2,1,0:T(8,128)(2,1)}) %all-gather.10.cloned.1.call-update) | async-done | bytes 4194320 | tf_op jit(solution)/shard_map/all_gather | solution.py:14
  217.1 55.0 %while.23 = (s32[]{:T(128)}, f32[1,2,128,128]{3,2,1,0:T(8,128)S(1)}, s32[]{:T(128)}, bf16[64,1,2,128,128]{4,3,2,1,0:T(8,128)(2,1)}, s32[]{:T(128)}, /*index=5*/s32[]{:T(128)}, s32[]{:T(128)}, s32[]{:T(128)}) while((s32[]{:T(128)}, f32[1,2,128,128]{3,2,1,0:T(8,128)S(1)}, s32[]{:T(128)}, bf16[64,1,2,128,128]{4,3,2,1,0:T(8,128)(2,1)}, s32[]{:T(128)}, ...), condition=%wide.region_3.4_spmd, body=%wide.region_2.3_spmd.sunk | while | flops 65542 | bytes 327823 | solution.py:21
  272.1 2.9 fusion.20
  276.6 25.6 %all-gather.8.cloned.1.call-done = bf16[128,128,128]{2,1,0:T(8,128)(2,1)} async-done(((bf16[2,128,128]{2,1,0:T(8,128)(2,1)}), bf16[128,128,128]{2,1,0:T(8,128)(2,1)}) %all-gather.8.cloned.1.call-update) | async-done | bytes 4194320 | tf_op jit(solution)/shard_map/all_gather | solution.py:14
  304.9 81.9 %all-gather.6.cloned.1.call-done = bf16[2048,768]{1,0:T(8,128)(2,1)} async-done(((bf16[32,768]{1,0:T(8,128)(2,1)}), bf16[2048,768]{1,0:T(8,128)(2,1)}) %all-gather.6.cloned.1.call-update) | async-done | bytes 3145744 | tf_op jit(solution)/shard_map/all_gather | solution.py:30
  386.8 6.9 %convert_bitcast_fusion = bf16[1024,1,2048]{2,0,1:T(8,128)(2,1)} fusion(bf16[1024,768]{0,1:T(8,128)(2,1)S(1)} %bitcast.111, bf16[2048,768]{1,0:T(8,128)(2,1)} %all-gather.6.cloned.1.call-done), kind=kOutput, calls=%fused_computation.8 | convolution fusion | flops 3223322624 | bytes 8912896 | tf_op jit(solution)/shard_map/stf,df->tsd/dot_general | solution.py:80
  393.8 54.2 %reduce-scatter.2.cloned.1.call-done = bf16[128,1,2048]{2,0,1:T(8,128)(2,1)} async-done(((bf16[1024,1,2048]{2,0,1:T(8,128)(2,1)}), bf16[128,1,2048]{2,0,1:T(8,128)(2,1)}) %reduce-scatter.2.cloned.1.call-update) | async-done | bytes 524304 | tf_op jit(solution)/shard_map/reduce_scatter | solution.py:79
  448.0 2.1 bitcast_convert_fusion
  (97 shorter events, 66.5 us)
Async XLA Ops:
  21.8 52.5 %all-to-all-start = ((bf16[8,2,16384]{2,1,0:T(2,128)(2,1)}), bf16[8,2,16384]{2,1,0:T(2,128)(2,1)}, u32[]{:S(2)}, u32[]{:S(2)}) async-start(bf16[8,2,16384]{2,1,0:T(2,128)(2,1)} %reshape.156), calls=%async_computation | async-start | bytes 1048576 | tf_op jit(solution)/shard_map/all_to_all | solution.py:33
  74.3 44.2 %all-to-all-start.1 = ((bf16[8,2,49152]{2,1,0:T(2,128)(2,1)}), bf16[8,2,49152]{2,1,0:T(2,128)(2,1)}, u32[]{:S(2)}, u32[]{:S(2)}) async-start(bf16[8,2,49152]{2,1,0:T(2,128)(2,1)} %reshape.158), calls=%async_computation.1 | async-start | bytes 3145728 | tf_op jit(solution)/shard_map/all_to_all | solution.py:32
  80.9 136.1 %all-gather.10.cloned.1.call-start = ((), (), s32[]{:S(2)}) async-start(), calls=%async_computation.6 | async-start | bytes 4259840 | tf_op jit(solution)/shard_map/all_gather | solution.py:14
  123.4 4.7 %copy-start = (bf16[1024,2,128]{0,2,1:T(8,128)(2,1)S(1)}, bf16[1024,2,128]{0,2,1:T(8,128)(2,1)}, u32[]{:S(2)}) copy-start(bf16[1024,2,128]{0,2,1:T(8,128)(2,1)} %reshape.144) | copy-start | bytes 1572868
  129.1 173.1 %all-gather.8.cloned.1.call-start = ((), (), s32[]{:S(2)}) async-start(), calls=%async_computation.5 | async-start | bytes 4259840 | tf_op jit(solution)/shard_map/all_gather | solution.py:14
  130.1 256.7 %all-gather.6.cloned.1.call-start = ((), (), s32[]{:S(2)}) async-start(), calls=%async_computation.3 | async-start | bytes 3194880 | tf_op jit(solution)/shard_map/all_gather | solution.py:30
  130.8 317.2 %reduce-scatter.2.cloned.1.call-start = ((), (), s32[]{:S(2)}) async-start(), calls=%async_computation.4 | async-start | bytes 4718592 | tf_op jit(solution)/shard_map/reduce_scatter | solution.py:79
  272.1 2.9 copy-start.1
  276.6 27.2 %copy-start.2 = (f32[1,1024,2,1,128]{1,4,2,3,0:T(8,128)S(1)}, f32[1,1024,2,1,128]{1,4,2,3,0:T(8,128)}, u32[]{:S(2)}) copy-start(f32[1,1024,2,1,128]{1,4,2,3,0:T(8,128)} %fusion.20) | copy-start | bytes 3145732
  303.1 1.2 copy-start.3
Sparse Core Ops, SparseCore 0:
  129.2 87.7 all-gather.9
  220.4 81.7 all-gather.7
  305.6 81.2 all-gather.5
  393.9 54.0 reduce-scatter.1
where the time goes:
time: 460 us; the launch traced here: 457 us
  waiting for transfers between devices  259 us (56%)
  other arithmetic  103 us (22%)
  matrix products  37.1 us (8%)
  local copies, waits for them, and re-layouts  28.3 us (6%)
  starting transfers between devices  14.6 us (3%)
  between operations  13.3 us (3%)
    all_gather x2, waiting for transfers between devices, carried_in(): gathered = lax.all_gather(x.astype(jnp.bfloat16), axis)  88.1 us
    all_gather x1, waiting for transfers between devices, per_device(): whole_weight = lax.all_gather(w_qkv, 'ctx', axis=0, tiled=True)  81.9 us
    add x63, other arithmetic, combine_sum(): return earlier + later  54.4 us
    reduce_scatter x1, waiting for transfers between devices, per_device(): lax.psum_scatter(jnp.einsum('stf,df->tsd', gradients, whole_weight, prefe...  54.2 us
    unnamed x2, other arithmetic  45.8 us
    all_to_all x1, waiting for transfers between devices, per_device(): lax.all_to_all(qkv, 'head', split_axis=2, concat_axis=1, tiled=True)  33.7 us
    unnamed x17, local copies, waits for them, and re-layouts  22.1 us
  transfers between devices with their start and end apart: 6, of which 5 were waited for; matrix products, arithmetic and copies ran while one was open for 29% of the time, Pallas kernels for 0%

commit v1 on v0

--- a/solution.py
+++ b/solution.py
@@ -5,6 +5,30 @@
 from jax.sharding import PartitionSpec as P
 
 DH = 128
+
+
+def cut_along(array, dim, size):
+    before, after = (array.shape[:dim], array.shape[dim + 1 :])
+    return jnp.moveaxis(array.reshape(*before, size, -1, *after), dim, 0)
+
+
+def in_order(blocks, dim):
+    blocks = jnp.moveaxis(blocks, 0, dim)
+    shape = blocks.shape
+    return blocks.reshape(*shape[:dim], shape[dim] * shape[dim + 1], *shape[dim + 2 :])
+
+
+def sent_to_each(shard, axis, split_dim, concat_dim):
+    devices, position = (lax.axis_size(axis), lax.axis_index(axis))
+    blocks = cut_along(shard, split_dim, devices)
+    gathered = [blocks[position]]
+    for step in range(1, devices):
+        sent = blocks[(position + step) % devices]
+        gathered.append(
+            lax.ppermute(sent, axis, [(i, (i + step) % devices) for i in range(devices)])
+        )
+    blocks = jnp.stack(gathered)[(position - jnp.arange(devices)) % devices]
+    return in_order(blocks, concat_dim)
 
 
 def carried_in(x, axis, join, neutral, backward):
@@ -29,7 +53,7 @@
     highest = lax.Precision.HIGHEST
     whole_weight = lax.all_gather(w_qkv, "ctx", axis=0, tiled=True)
     local_qkv, local_grad = (
-        lax.all_to_all(qkv, "head", split_axis=2, concat_axis=1, tiled=True),
+        sent_to_each(qkv, "head", 2, 1),
         lax.all_to_all(grad_out, "head", split_axis=2, concat_axis=1, tiled=True),
     )
     num_seqs, block_len, width3 = local_qkv.shape

time: 460 us -> 397 us (0.86)
  waiting for transfers between devices: 259 us -> 216 us
  other arithmetic: 103 us -> 69 us
  blocking collectives: 0 us -> 20.8 us
  local copies, waits for them, and re-layouts: 28.3 us -> 11.5 us
  starting transfers between devices: 14.6 us -> 29.5 us
  matrix products: 37.1 us -> 32.3 us
    all_gather x1, waiting for transfers between devices: 81.9 us -> 25.9 us  [per_device(): whole_weight = lax.all_gather(w_qkv, 'ctx', axis=0, tiled=True)]
    unnamed x2 -> x1, other arithmetic: 45.8 us -> 11.5 us
    all_to_all x2 -> x0, waiting for transfers between devices: 33.7 us -> none  [the longest x1 33.7 us: per_device(): lax.all_to_all(qkv, 'head', split_axis=2, concat_axis=1, tiled=True)]
    ppermute x0 -> x7, starting transfers between devices: none -> 29.2 us  [sent_to_each(): lax.ppermute(sent, axis, [(i, (i + step) % devices) for i in range(device...]
    all_gather x2, waiting for transfers between devices: 88.1 us -> 114 us  [carried_in(): gathered = lax.all_gather(x.astype(jnp.bfloat16), axis)]
    ppermute x0 -> x7, waiting for transfers between devices: none -> 21.1 us  [sent_to_each(): lax.ppermute(sent, axis, [(i, (i + step) % devices) for i in range(device...]
    all_to_all x0 -> x1, blocking collectives: none -> 20.8 us  [per_device(): lax.all_to_all(grad_out, 'head', split_axis=2, concat_axis=1, tiled=True)]
    unnamed x17, local copies, waits for them, and re-layouts: 22.1 us -> 5.53 us
  transfers between devices with their start and end apart: 6 -> 11, of which waited for: 5 -> 8; matrix products, arithmetic and copies ran while one was open for 29% -> 25% of each run, Pallas kernels for 0% -> 0%
where the time goes in v1:
time: 397 us; the launch traced here: 394 us
  waiting for transfers between devices  216 us (54%)
  other arithmetic  69 us (17%)
  matrix products  32.3 us (8%)
  starting transfers between devices  29.5 us (7%)
  blocking collectives  20.8 us (5%)
  between operations  13.5 us (3%)
  local copies, waits for them, and re-layouts  11.5 us (3%)
    all_gather x2, waiting for transfers between devices, carried_in(): gathered = lax.all_gather(x.astype(jnp.bfloat16), axis)  114 us
    add x63, other arithmetic, combine_sum(): return earlier + later  54.4 us
    reduce_scatter x1, waiting for transfers between devices, per_device(): lax.psum_scatter(jnp.einsum('stf,df->tsd', gradients, whole_weight, prefe...  54.2 us
    ppermute x7, starting transfers between devices, sent_to_each(): lax.ppermute(sent, axis, [(i, (i + step) % devices) for i in range(device...  29.2 us
    all_gather x1, waiting for transfers between devices, per_device(): whole_weight = lax.all_gather(w_qkv, 'ctx', axis=0, tiled=True)  25.9 us
    ppermute x7, waiting for transfers between devices, sent_to_each(): lax.ppermute(sent, axis, [(i, (i + step) % devices) for i in range(device...  21.1 us
    all_to_all x1, blocking collectives, per_device(): lax.all_to_all(grad_out, 'head', split_axis=2, concat_axis=1, tiled=True)  20.8 us
    unnamed x1, other arithmetic  11.5 us
  transfers between devices with their start and end apart: 11, of which 8 were waited for; matrix products, arithmetic and copies ran while one was open for 25% of the time, Pallas kernels for 0%

profile of v1, /device:TPU:1, one launch (start us, length us, event | category | flops | bytes accessed | tf_op | source)
XLA Modules:
  0.0 393.9 jit_solution(6660177932900978213)
XLA Ops:
  9.5 4.0 %collective-permute-start = (bf16[1,128,768]{2,1,0:T(8,128)(2,1)}, bf16[1,128,768]{2,1,0:T(8,128)(2,1)}, u32[]{:S(2)}, u32[]{:S(2)}) collective-permute-start(bf16[1,128,768]{2,1,0:T(8,128)(2,1)} %bitcast.4), channel_id=1, source_target_pairs={{0,1},{1,2},{2,3},{3,4},{4,5},{5,6},{6,7},{7,0},{8,9},{9,10},{10,1... | collective-permute-start | bytes 589832 | tf_op jit(solution)/shard_map/ppermute | solution.py:28
  14.3 4.2 %collective-permute-start.1 = (bf16[1,128,768]{2,1,0:T(8,128)(2,1)}, bf16[1,128,768]{2,1,0:T(8,128)(2,1)S(1)}, u32[]{:S(2)}, u32[]{:S(2)}) collective-permute-start(bf16[1,128,768]{2,1,0:T(8,128)(2,1)} %bitcast.6), channel_id=1, source_target_pairs={{0,2},{1,3},{2,4},{3,5},{4,6},{5,7},{6,0},{7,1},{8,10},{9,11},{10,... | collective-permute-start | bytes 589832 | tf_op jit(solution)/shard_map/ppermute | solution.py:28
  18.7 4.6 %collective-permute-start.2 = (bf16[1,128,768]{2,1,0:T(8,128)(2,1)S(1)}, bf16[1,128,768]{2,1,0:T(8,128)(2,1)S(1)}, u32[]{:S(2)}, u32[]{:S(2)}) collective-permute-start(bf16[1,128,768]{2,1,0:T(8,128)(2,1)S(1)} %bitcast.134), channel_id=1, source_target_pairs={{0,3},{1,4},{2,5},{3,6},{4,7},{5,0},{6,1},{7,2},{8,11},{9,12},{10,... | collective-permute-start | bytes 589832 | tf_op jit(solution)/shard_map/ppermute | solution.py:28
  23.5 3.5 collective-permute-start.3
  27.2 4.9 %collective-permute-start.4 = (bf16[1,128,768]{2,1,0:T(8,128)(2,1)S(1)}, bf16[1,128,768]{2,1,0:T(8,128)(2,1)S(1)}, u32[]{:S(2)}, u32[]{:S(2)}) collective-permute-start(bf16[1,128,768]{2,1,0:T(8,128)(2,1)S(1)} %bitcast.132), channel_id=1, source_target_pairs={{0,5},{1,6},{2,7},{3,0},{4,1},{5,2},{6,3},{7,4},{8,13},{9,14},{10,... | collective-permute-start | bytes 589832 | tf_op jit(solution)/shard_map/ppermute | solution.py:28
  32.6 5.0 %collective-permute-start.5 = (bf16[1,128,768]{2,1,0:T(8,128)(2,1)S(1)}, bf16[1,128,768]{2,1,0:T(8,128)(2,1)S(1)}, u32[]{:S(2)}, u32[]{:S(2)}) collective-permute-start(bf16[1,128,768]{2,1,0:T(8,128)(2,1)S(1)} %bitcast.135), channel_id=1, source_target_pairs={{0,6},{1,7},{2,0},{3,1},{4,2},{5,3},{6,4},{7,5},{8,14},{9,15},{10,... | collective-permute-start | bytes 589832 | tf_op jit(solution)/shard_map/ppermute | solution.py:28
  38.5 3.0 collective-permute-start.6
  41.5 6.1 %collective-permute-done.3 = bf16[1,128,768]{2,1,0:T(8,128)(2,1)S(1)} collective-permute-done((bf16[1,128,768]{2,1,0:T(8,128)(2,1)S(1)}, bf16[1,128,768]{2,1,0:T(8,128)(2,1)S(1)}, u32[]{:S(2)}, u32[]{:S(2)}) %collective-permute-start.3) | collective-permute-done | bytes 196640 | tf_op jit(solution)/shard_map/ppermute | solution.py:28
  47.6 3.3 collective-permute-done.4
  51.0 9.5 %collective-permute-done.5 = bf16[1,128,768]{2,1,0:T(8,128)(2,1)S(1)} collective-permute-done((bf16[1,128,768]{2,1,0:T(8,128)(2,1)S(1)}, bf16[1,128,768]{2,1,0:T(8,128)(2,1)S(1)}, u32[]{:S(2)}, u32[]{:S(2)}) %collective-permute-start.5) | collective-permute-done | bytes 196640 | tf_op jit(solution)/shard_map/ppermute | solution.py:28
  60.6 2.1 collective-permute-done.6
  67.6 11.5 %reduce = bf16[2048,128]{1,0:T(8,128)(2,1)S(1)} reduce(bf16[2048,1,128]{2,1,0:T(2,128)(2,1)S(1)} %bitcast.127, bf16[]{:T(256)} %broadcast.85), dimensions={1}, to_apply=%bitcast.113.reduce_sub_computation | reduce | bytes 1048578
  79.3 20.8 %all_to_all.15 = bf16[8,2,16384]{2,1,0:T(2,128)(2,1)S(1)} all-to-all(bf16[8,2,16384]{2,1,0:T(2,128)(2,1)S(1)} %reshape.226), channel_id=1, replica_groups=mesh['ctx'=64,'head'=8] {'head'}, dimensions={0} | all-to-all | bytes 1048576 | tf_op jit(solution)/shard_map/all_to_all | solution.py:57
  106.3 5.0 %fusion.2 = f32[2,128,1024]{2,1,0:T(8,128)S(1)} fusion(f32[2,1024,1024]{2,1,0:T(8,128)S(1)} %fusion.15, f32[1024,1024]{0,1:T(8,128)S(1)} %fusion.7, bf16[1,1024,2,3,128]{1,4,3,2,0:T(8,128)(2,1)S(1)} %reshape_reshape_transpose.3), kind=kOutput, calls=%fused_computation.6 | convolution fusion | flops 3223322624 | bytes 14155776 | tf_op jit(solution)/shard_map/shtu,sthd->suhd/dot_general | solution.py:92
  111.3 4.4 %fusion.3 = f32[2,128,1024]{2,1,0:T(8,128)} fusion(f32[2,1024,1024]{2,1,0:T(8,128)S(1)} %fusion.15, f32[1024,1024]{0,1:T(8,128)S(1)} %fusion.7, bf16[1,1024,2,3,128]{1,4,3,2,0:T(8,128)(2,1)S(1)} %reshape_reshape_transpose.3), kind=kOutput, calls=%fused_computation.7 | convolution fusion | flops 3223322624 | bytes 14155776 | tf_op jit(solution)/shard_map/shtu,suhd->sthd/dot_general | solution.py:87
  115.7 6.2 %fusion.9 = f32[2,128,1024]{2,1,0:T(8,128)} fusion(bf16[1024,2,128]{0,2,1:T(8,128)(2,1)S(1)} %reshape.206, f32[2,1024,1024]{1,2,0:T(8,128)S(1)} %fusion.16, f32[1024,1024]{0,1:T(8,128)S(1)} %fusion.7), kind=kOutput, calls=%fused_computation.16 | convolution fusion | flops 3223322624 | bytes 14155776 | tf_op jit(solution)/shard_map/shtu,sthe->suhe/dot_general | solution.py:95
  121.9 32.3 %all-gather.8.cloned.1.call-done = bf16[128,128,128]{2,1,0:T(8,128)(2,1)} async-done(((bf16[2,128,128]{2,1,0:T(8,128)(2,1)}), bf16[128,128,128]{2,1,0:T(8,128)(2,1)}) %all-gather.8.cloned.1.call-update) | async-done | bytes 4194320 | tf_op jit(solution)/shard_map/all_gather | solution.py:38
  155.2 2.8 fusion.14
  158.0 81.5 %all-gather.10.cloned.1.call-done = bf16[128,128,128]{2,1,0:T(8,128)(2,1)} async-done(((bf16[2,128,128]{2,1,0:T(8,128)(2,1)}), bf16[128,128,128]{2,1,0:T(8,128)(2,1)}) %all-gather.10.cloned.1.call-update) | async-done | bytes 4194320 | tf_op jit(solution)/shard_map/all_gather | solution.py:38
  239.5 55.0 %while.23 = (s32[]{:T(128)}, f32[1,2,128,128]{3,2,1,0:T(8,128)S(1)}, s32[]{:T(128)}, bf16[64,1,2,128,128]{4,3,2,1,0:T(8,128)(2,1)}, s32[]{:T(128)}, /*index=5*/s32[]{:T(128)}, s32[]{:T(128)}, s32[]{:T(128)}) while((s32[]{:T(128)}, f32[1,2,128,128]{3,2,1,0:T(8,128)S(1)}, s32[]{:T(128)}, bf16[64,1,2,128,128]{4,3,2,1,0:T(8,128)(2,1)}, s32[]{:T(128)}, ...), condition=%wide.region_3.4_spmd, body=%wide.region_2.3_spmd.sunk | while | flops 65542 | bytes 327823 | solution.py:45
  298.1 25.9 %all-gather.6.cloned.1.call-done = bf16[2048,768]{1,0:T(8,128)(2,1)} async-done(((bf16[32,768]{1,0:T(8,128)(2,1)}), bf16[2048,768]{1,0:T(8,128)(2,1)}) %all-gather.6.cloned.1.call-update) | async-done | bytes 3145744 | tf_op jit(solution)/shard_map/all_gather | solution.py:54
  324.0 6.9 %convert_bitcast_fusion = bf16[1024,1,2048]{2,0,1:T(8,128)(2,1)} fusion(bf16[1024,768]{0,1:T(8,128)(2,1)S(1)} %bitcast.130, bf16[2048,768]{1,0:T(8,128)(2,1)} %all-gather.6.cloned.1.call-done), kind=kOutput, calls=%fused_computation.8 | convolution fusion | flops 3223322624 | bytes 8912896 | tf_op jit(solution)/shard_map/stf,df->tsd/dot_general | solution.py:104
  331.0 54.2 %reduce-scatter.2.cloned.1.call-done = bf16[128,1,2048]{2,0,1:T(8,128)(2,1)} async-done(((bf16[1024,1,2048]{2,0,1:T(8,128)(2,1)}), bf16[128,1,2048]{2,0,1:T(8,128)(2,1)}) %reduce-scatter.2.cloned.1.call-update) | async-done | bytes 524304 | tf_op jit(solution)/shard_map/reduce_scatter | solution.py:103
  385.2 2.1 bitcast_convert_fusion
  (120 shorter events, 75.7 us)
Async XLA Ops:
  6.5 147.7 %all-gather.8.cloned.1.call-start = ((), (), s32[]{:S(2)}) async-start(), calls=%async_computation.4 | async-start | bytes 4259840 | tf_op jit(solution)/shard_map/all_gather | solution.py:38
  9.5 23.1 %collective-permute-start = (bf16[1,128,768]{2,1,0:T(8,128)(2,1)}, bf16[1,128,768]{2,1,0:T(8,128)(2,1)}, u32[]{:S(2)}, u32[]{:S(2)}) collective-permute-start(bf16[1,128,768]{2,1,0:T(8,128)(2,1)} %bitcast.4), channel_id=1, source_target_pairs={{0,1},{1,2},{2,3},{3,4},{4,5},{5,6},{6,7},{7,0},{8,9},{9,10},{10,1... | collective-permute-start | bytes 589832 | tf_op jit(solution)/shard_map/ppermute | solution.py:28
  14.3 24.2 %collective-permute-start.1 = (bf16[1,128,768]{2,1,0:T(8,128)(2,1)}, bf16[1,128,768]{2,1,0:T(8,128)(2,1)S(1)}, u32[]{:S(2)}, u32[]{:S(2)}) collective-permute-start(bf16[1,128,768]{2,1,0:T(8,128)(2,1)} %bitcast.6), channel_id=1, source_target_pairs={{0,2},{1,3},{2,4},{3,5},{4,6},{5,7},{6,0},{7,1},{8,10},{9,11},{10,... | collective-permute-start | bytes 589832 | tf_op jit(solution)/shard_map/ppermute | solution.py:28
  18.7 22.8 %collective-permute-start.2 = (bf16[1,128,768]{2,1,0:T(8,128)(2,1)S(1)}, bf16[1,128,768]{2,1,0:T(8,128)(2,1)S(1)}, u32[]{:S(2)}, u32[]{:S(2)}) collective-permute-start(bf16[1,128,768]{2,1,0:T(8,128)(2,1)S(1)} %bitcast.134), channel_id=1, source_target_pairs={{0,3},{1,4},{2,5},{3,6},{4,7},{5,0},{6,1},{7,2},{8,11},{9,12},{10,... | collective-permute-start | bytes 589832 | tf_op jit(solution)/shard_map/ppermute | solution.py:28
  23.5 24.1 %collective-permute-start.3 = (bf16[1,128,768]{2,1,0:T(8,128)(2,1)S(1)}, bf16[1,128,768]{2,1,0:T(8,128)(2,1)S(1)}, u32[]{:S(2)}, u32[]{:S(2)}) collective-permute-start(bf16[1,128,768]{2,1,0:T(8,128)(2,1)S(1)} %bitcast.133), channel_id=1, source_target_pairs={{0,4},{1,5},{2,6},{3,7},{4,0},{5,1},{6,2},{7,3},{8,12},{9,13},{10,... | collective-permute-start | bytes 589832 | tf_op jit(solution)/shard_map/ppermute | solution.py:28
  27.2 23.8 %collective-permute-start.4 = (bf16[1,128,768]{2,1,0:T(8,128)(2,1)S(1)}, bf16[1,128,768]{2,1,0:T(8,128)(2,1)S(1)}, u32[]{:S(2)}, u32[]{:S(2)}) collective-permute-start(bf16[1,128,768]{2,1,0:T(8,128)(2,1)S(1)} %bitcast.132), channel_id=1, source_target_pairs={{0,5},{1,6},{2,7},{3,0},{4,1},{5,2},{6,3},{7,4},{8,13},{9,14},{10,... | collective-permute-start | bytes 589832 | tf_op jit(solution)/shard_map/ppermute | solution.py:28
  32.6 28.0 %collective-permute-start.5 = (bf16[1,128,768]{2,1,0:T(8,128)(2,1)S(1)}, bf16[1,128,768]{2,1,0:T(8,128)(2,1)S(1)}, u32[]{:S(2)}, u32[]{:S(2)}) collective-permute-start(bf16[1,128,768]{2,1,0:T(8,128)(2,1)S(1)} %bitcast.135), channel_id=1, source_target_pairs={{0,6},{1,7},{2,0},{3,1},{4,2},{5,3},{6,4},{7,5},{8,14},{9,15},{10,... | collective-permute-start | bytes 589832 | tf_op jit(solution)/shard_map/ppermute | solution.py:28
  38.5 24.2 %collective-permute-start.6 = (bf16[1,128,768]{2,1,0:T(8,128)(2,1)S(1)}, bf16[1,128,768]{2,1,0:T(8,128)(2,1)S(1)}, u32[]{:S(2)}, u32[]{:S(2)}) collective-permute-start(bf16[1,128,768]{2,1,0:T(8,128)(2,1)S(1)} %bitcast.131), channel_id=1, source_target_pairs={{0,7},{1,0},{2,1},{3,2},{4,3},{5,4},{6,5},{7,6},{8,15},{9,8},{10,9... | collective-permute-start | bytes 589832 | tf_op jit(solution)/shard_map/ppermute | solution.py:28
  65.3 1.0 copy-start.1
  66.3 173.2 %all-gather.10.cloned.1.call-start = ((), (), s32[]{:S(2)}) async-start(), calls=%async_computation.5 | async-start | bytes 4259840 | tf_op jit(solution)/shard_map/all_gather | solution.py:38
  102.2 221.8 %all-gather.6.cloned.1.call-start = ((), (), s32[]{:S(2)}) async-start(), calls=%async_computation.2 | async-start | bytes 3194880 | tf_op jit(solution)/shard_map/all_gather | solution.py:54
  103.0 282.3 %reduce-scatter.2.cloned.1.call-start = ((), (), s32[]{:S(2)}) async-start(), calls=%async_computation.3 | async-start | bytes 4718592 | tf_op jit(solution)/shard_map/reduce_scatter | solution.py:103
  296.3 1.2 copy-start
Sparse Core Ops, SparseCore 0:
  66.4 87.8 all-gather.7
  157.6 81.7 all-gather.9
  242.8 81.2 all-gather.5
  331.1 54.0 reduce-scatter.1
